TPU v7x, 32 devices: a whole 2x2x4 slice. The times are simulated.
32 devices in a mesh: lat: 4 (over x, core), lon: 8 (over z, y).
Axes of the slice: x: 2, y: 2, z: 4, core: 2. Of those that a mesh axis runs over, the one named last changes fastest.
Arguments:
- latent_field: float32 [32, 8, 64, 1024], P(None, None, 'lat', 'lon'), may hold values from -6 to 6
- east_courant: float32 [8, 64, 1024], P(None, 'lat', 'lon'), may hold values from -0.45 to 0.45
- north_courant: float32 [8, 64, 1024], P(None, 'lat', 'lon'), may hold values from -0.45 to 0.45
- mixing: float32 [7, 64, 1024], P(None, 'lat', 'lon'), may hold values from 0.2 to 5
- sunlit: int32 [4, 64], P('lat', 'lon'), may hold values from 0 to 1, as said below
- decode_w: bfloat16 [224, 32], replicated, may hold values from -1 to 1
- react_a: bfloat16 [256, 224], replicated, may hold values from -0.375 to 0.375
- react_b: bfloat16 [256, 224], replicated, may hold values from -0.375 to 0.375
- stoich: bfloat16 [224, 256], replicated, may hold values from -0.375 to 0.375
- encode_w: bfloat16 [32, 224], replicated, may hold values from -0.375 to 0.375
- rate_const: float32 [256], replicated, may hold values from 0.05 to 0.5
Outputs:
- advanced: float32 [32, 8, 64, 1024], P(None, None, 'lat', 'lon')
Inputs may be any that keep to these rules, and one draw needn't show every extreme that they name: In each row of blocks the sunlit blocks form one run, periodic in longitude, of 16 to 48 blocks.
All inputs are finite; a program needn't handle non-finite values.
Results may differ from a plain program's by a relative error of at most 0.0035.
Values may be sent and summed in bfloat16 or wider, within the bound.
No kernel may reach another device: no remote copies, remote signals or barrier semaphores. Data moves between devices by JAX's collectives and lax.ppermute only.
A program may use at most 128 MiB of HBM per device.

v0:
```python
import functools
import itertools

import jax
import jax.numpy as jnp
from jax import lax
from jax.experimental import pallas as pl
from jax.experimental.pallas import tpu as pltpu
from jax.sharding import PartitionSpec as P

BLOCK = 16
SUBSTEPS = 2
STEPS = 2
GROUP = 16
ROWS_AT_ONCE = 4
LEVELS_AT_ONCE = 4
LAG = 2

F32 = jnp.float32
BF16 = jnp.bfloat16
VMEM_BYTES = 48 * 1024 * 1024
FIRST_VMEM_BYTES = 56 * 1024 * 1024


def lane_ids(shape):
    return lax.broadcasted_iota(jnp.int32, shape, len(shape) - 1)


def fold_weights(decode_t, react_a_t, react_b_t, stoich, encode, rate, linear_out, encode_out):
    n_reactions = react_a_t.shape[1]
    contract = (((0,), (1,)), ((), ()))
    for part, react in enumerate((react_a_t, react_b_t)):
        product = lax.dot_general(
            react[...], decode_t[...], contract, preferred_element_type=F32
        )
        for group in range(n_reactions // GROUP):
            at = (2 * group + part) * GROUP
            linear_out[at : at + GROUP, :] = product[
                group * GROUP : (group + 1) * GROUP
            ].astype(BF16)
    folded = jnp.dot(encode[...], stoich[...], preferred_element_type=F32)
    encode_out[...] = (folded * rate[...]).astype(BF16)


def at_ends():
    index = lax.axis_index("lat")
    return index == 0, index == lax.axis_size("lat") - 1


def pack_sides(value, coef, at, west, east):
    lanes = lane_ids(value.shape)
    size = value.shape[-1]
    turned = pltpu.roll(value * coef, at, 1)
    west = jnp.where(lanes == at, turned, west)
    east = jnp.where(lanes == (at + size - 1) % size, turned, east)
    return west, east


def first_kernel(latent, east_c, north_c, west, east, south, north, *scratch):
    tiles, east_v, north_v, sems = scratch
    n_levels, n_species, n_rows, n_cols = tiles.shape
    lanes = lane_ids((1, n_cols))
    is_first, is_last = at_ends()
    copies = [
        pltpu.make_async_copy(east_c, east_v, sems.at[n_levels]),
        pltpu.make_async_copy(north_c, north_v, sems.at[n_levels + 1]),
    ]
    levels = [
        pltpu.make_async_copy(latent.at[:, level], tiles.at[level], sems.at[level])
        for level in range(n_levels)
    ]
    for copy in copies + levels:
        copy.start()
    for copy in copies:
        copy.wait()
    sides = (jnp.zeros((n_species, n_cols), F32),) * 2
    for level in range(n_levels):
        levels[level].wait()
        tile = jnp.transpose(tiles[level], (1, 0, 2))
        for r in range(n_rows):
            at = level * n_rows + r
            value = tile[r]
            speed = east_v[level, r : r + 1, :]
            coef = jnp.where(lanes == 0, jnp.minimum(speed, 0.0), jnp.maximum(speed, 0.0))
            sides = pack_sides(value, coef, at, *sides)
        for r, out, clip in ((0, south, jnp.minimum), (n_rows - 1, north, jnp.maximum)):
            speed = clip(north_v[level, r : r + 1, :], 0.0)
            speed = jnp.where(is_first if r == 0 else is_last, 0.0, speed)
            out[level] = (tile[r] * speed).astype(BF16)
    west[...], east[...] = sides


def step_kernel(
    n_levels,
    n_rows,
    first,
    last,
    sun,
    field,
    east_c,
    north_c,
    mixing,
    west_in,
    east_in,
    south_in,
    north_in,
    *refs,
):
    if first:
        weights, refs = refs[:6], refs[6:]
        linear, encode = refs[5:7]
    else:
        (linear, encode), refs = refs[:2], refs[2:]
    half_rows = n_rows // 2
    if last:
        coefs, diffused, staged, sems = refs[-4:]
    else:
        coefs, diffused = refs[-2:]
    n_species, n_cols = west_in.shape
    n_reactions = encode.shape[1]
    cells = n_levels * n_rows
    lanes = lane_ids((1, n_cols))
    row_ids = lax.broadcasted_iota(jnp.int32, (n_rows, n_cols), 0)
    is_first, is_last = at_ends()
    if first:
        latent, field = field, refs[-3]
        fold_weights(*weights, linear, encode)
        for level in range(n_levels):
            field[level] = jnp.transpose(latent[:, level], (1, 0, 2))
    CENTRE, EAST, WEST, NORTH, SOUTH, SCALE, LOWER, UPPER = range(8)

    upper = None
    for level in range(n_levels):
        ce, cn = east_c[level], north_c[level]
        east, west = jnp.maximum(ce, 0.0), jnp.minimum(ce, 0.0)
        north = jnp.where((row_ids == n_rows - 1) & is_last, 0.0, jnp.maximum(cn, 0.0))
        south = jnp.where((row_ids == 0) & is_first, 0.0, jnp.minimum(cn, 0.0))
        coefs[CENTRE, level] = 1.0 - east + west - north + south
        coefs[EAST, level] = east
        coefs[WEST, level] = west
        coefs[NORTH, level] = north
        coefs[SOUTH, level] = south
        pivot = 1.0
        if level > 0:
            below = mixing[level - 1]
            pivot = pivot + below - below * upper
        if level < n_levels - 1:
            pivot = pivot + mixing[level]
        scale = 1.0 / pivot
        coefs[SCALE, level] = scale
        if level > 0:
            coefs[LOWER, level] = below * scale
        if level < n_levels - 1:
            upper = mixing[level] * scale
            coefs[UPPER, level] = upper

    lit = jnp.zeros((1, n_cols), jnp.int32)
    for block in range(n_cols // BLOCK):
        lit = jnp.where(lanes // BLOCK == block, sun[0, block], lit)
    lit = lit > 0

    def coef(kind, level, r):
        return coefs[kind, level, pl.ds(r, 1), :]

    def transport(slot):
        r = jnp.minimum(slot, n_rows - 1)
        before, after = jnp.maximum(r - 1, 0), jnp.minimum(r + 1, n_rows - 1)
        right = None
        for level in range(n_levels):
            at = level * n_rows + r
            value = field[level, r]
            from_west = jnp.where(
                lanes == 0,
                pltpu.roll(west_in[...], (n_cols + 1 - at) % n_cols, 1),
                pltpu.roll(value * coef(EAST, level, r), 1, 1),
            )
            from_east = jnp.where(
                lanes == n_cols - 1,
                pltpu.roll(east_in[...], n_cols - 1 - at, 1),
                pltpu.roll(value * coef(WEST, level, r), n_cols - 1, 1),
            )
            from_south = jnp.where(
                r == 0,
                south_in[level].astype(F32),
                field[level, before] * coef(NORTH, level, before),
            )
            from_north = jnp.where(
                r == n_rows - 1,
                north_in[level].astype(F32),
                field[level, after] * coef(SOUTH, level, after),
            )
            moved = value * coef(CENTRE, level, r) + (from_west - from_east) + (from_south - from_north)
            scaled = moved * coef(SCALE, level, r)
            right = scaled if level == 0 else scaled + coef(LOWER, level, r) * right
            diffused[level, slot] = right
            yield
        for level in range(n_levels - 2, -1, -1):
            right = diffused[level, slot] + coef(UPPER, level, r) * right
            diffused[level, slot] = right
            yield

    def product_of(rounded):
        both = jnp.dot(linear[...], rounded, preferred_element_type=F32)
        parts = [
            both[at : at + GROUP] * both[at + GROUP : at + 2 * GROUP]
            for at in range(0, 2 * n_reactions, 2 * GROUP)
        ]
        return jnp.concatenate(parts, axis=0).astype(BF16)

    def increments(rounded, beside):
        current = [value.astype(F32) for value in rounded]
        summed = [None] * len(rounded)
        units = [(substep, tile) for substep in range(SUBSTEPS) for tile in range(len(rounded))]
        rates = {}
        for at in range(len(units) + LAG):
            if at < len(units):
                rates[at] = product_of(rounded[units[at][1]])
                beside()
            if at >= LAG:
                substep, tile = units[at - LAG]
                change = jnp.dot(encode[...], rates.pop(at - LAG), preferred_element_type=F32)
                if substep == 0:
                    summed[tile] = change
                else:
                    summed[tile] = summed[tile] + change
                if substep < SUBSTEPS - 1:
                    current[tile] = current[tile] + change
                    rounded[tile] = current[tile].astype(BF16)
        return summed

    for r in range(ROWS_AT_ONCE):
        for _ in transport(r):
            pass
    lit_tile = jnp.concatenate([lit] * LEVELS_AT_ONCE, axis=1)

    def rows(group, sides):
        places = [
            (level, group * ROWS_AT_ONCE + extra)
            for extra in range(ROWS_AT_ONCE)
            for level in range(0, n_levels, LEVELS_AT_ONCE)
        ]

        def tile_at(level, r):
            return jnp.concatenate(
                [diffused[level + extra, r] for extra in range(LEVELS_AT_ONCE)], axis=1
            )

        rounded = [tile_at(*place).astype(BF16) for place in places]
        ahead = itertools.chain(
            *[transport((group + 1) * ROWS_AT_ONCE + extra) for extra in range(ROWS_AT_ONCE)]
        )
        steps = (2 * n_levels - 1) * ROWS_AT_ONCE
        share = -(-steps // (SUBSTEPS * len(places) - 1))

        def beside():
            for _ in itertools.islice(ahead, share):
                pass

        changes = increments(rounded, beside)
        for _ in ahead:
            pass
        for (level, r), change in zip(places, changes):
            tile = tile_at(level, r) + jnp.where(lit_tile, change, 0.0)
            for half in range(LEVELS_AT_ONCE):
                value = tile[:, half * n_cols : (half + 1) * n_cols]
                at = (level + half) * n_rows + r
                if last:
                    diffused[level + half, r] = value
                else:
                    refs[0][level + half, r] = value
                    speed = east_c[level + half, pl.ds(r, 1), :]
                    side = jnp.where(
                        lanes == 0, jnp.minimum(speed, 0.0), jnp.maximum(speed, 0.0)
                    )
                    sides = pack_sides(value, side, at, *sides)
        return sides

    n_groups = n_rows // ROWS_AT_ONCE
    if last:
        copies = []
        for half in range(2):
            lax.fori_loop(half * n_groups // 2, (half + 1) * n_groups // 2, rows, 0)
            within = slice(half * half_rows, (half + 1) * half_rows)
            for level in range(n_levels):
                staged[half, level] = jnp.transpose(diffused[level, within], (1, 0, 2))
                copies.append(
                    pltpu.make_async_copy(
                        staged.at[half, level],
                        refs[0].at[:, level, within],
                        sems.at[half, level],
                    )
                )
                copies[-1].start()
        for copy in copies:
            copy.wait()
        return
    out, west, east, south, north = refs[:5]
    zeros = jnp.zeros((n_species, n_cols), F32)
    west[...], east[...] = lax.fori_loop(0, n_groups, rows, (zeros, zeros))
    for level in range(n_levels):
        for edge, send, kind in ((0, south, SOUTH), (n_rows - 1, north, NORTH)):
            send[level] = (out[level, edge] * coefs[kind, level, edge : edge + 1]).astype(BF16)


def vmem(count):
    return [pl.BlockSpec(memory_space=pltpu.VMEM)] * count


def exchanged(west, east, south, north):
    lon, lat = lax.axis_size("lon"), lax.axis_size("lat")
    up = [(i, (i + 1) % lon) for i in range(lon)]
    down = [(j, i) for i, j in up]
    climb = [(i, (i + 1) % lat) for i in range(lat)]
    descend = [(j, i) for i, j in climb]
    from_south = lax.ppermute(north, "lat", climb)
    from_north = lax.ppermute(south, "lat", descend)
    from_west = lax.ppermute(east, "lon", up)
    from_east = lax.ppermute(west, "lon", down)
    return from_west, from_east, from_south, from_north


def on_device(
    latent_field,
    east_courant,
    north_courant,
    mixing,
    sunlit,
    decode_w,
    react_a,
    react_b,
    stoich,
    encode_w,
    rate_const,
):
    n_species, n_levels, n_rows, n_cols = latent_field.shape
    layered = jax.ShapeDtypeStruct((n_levels, n_rows, n_species, n_cols), F32)
    side = jax.ShapeDtypeStruct((n_species, n_cols), F32)
    edge = jax.ShapeDtypeStruct((n_levels, n_species, n_cols), BF16)
    params = pltpu.CompilerParams(vmem_limit_bytes=VMEM_BYTES)
    smem = pl.BlockSpec(memory_space=pltpu.SMEM)
    hbm = pl.BlockSpec(memory_space=pltpu.HBM)
    n_reactions = react_a.shape[0]
    edges = pl.pallas_call(
        first_kernel,
        out_shape=(side, side, edge, edge),
        in_specs=[hbm] * 3,
        out_specs=tuple(vmem(4)),
        scratch_shapes=[
            pltpu.VMEM((n_levels, n_species, n_rows, n_cols), F32),
            pltpu.VMEM((n_levels, n_rows, n_cols), F32),
            pltpu.VMEM((n_levels, n_rows, n_cols), F32),
            pltpu.SemaphoreType.DMA((n_levels + 2,)),
        ],
        compiler_params=pltpu.CompilerParams(vmem_limit_bytes=FIRST_VMEM_BYTES),
        name="first_sends",
        cost_estimate=pl.CostEstimate(flops=4_000_000_000, bytes_accessed=2_000_000, transcendentals=0),
    )(latent_field, east_courant, north_courant)
    weights = (decode_w.T, react_a.T, react_b.T, stoich, encode_w, rate_const[None])
    folded = (
        jax.ShapeDtypeStruct((2 * n_reactions, n_species), BF16),
        jax.ShapeDtypeStruct((n_species, n_reactions), BF16),
    )
    field = latent_field
    for step in range(STEPS):
        first, last = step == 0, step == STEPS - 1
        halos = exchanged(*edges)
        scratch = [pltpu.VMEM(layered.shape, F32)] if first else []
        scratch += [
            pltpu.VMEM((8, n_levels, n_rows, n_cols), F32),
            pltpu.VMEM((n_levels, n_rows + ROWS_AT_ONCE, n_species, n_cols), F32),
        ]
        if last:
            scratch += [
                pltpu.VMEM((2, n_levels, n_species, n_rows // 2, n_cols), F32),
                pltpu.SemaphoreType.DMA((2, n_levels)),
            ]
        outs = pl.pallas_call(
            functools.partial(step_kernel, n_levels, n_rows, first, last),
            out_shape=(jax.ShapeDtypeStruct(latent_field.shape, F32),)
            if last
            else (layered, side, side, edge, edge, *folded),
            in_specs=[smem] + vmem(8 + len(weights)),
            out_specs=(hbm,) if last else tuple(vmem(7)),
            scratch_shapes=scratch,
            compiler_params=params,
            name="splitting_step",
            cost_estimate=pl.CostEstimate(flops=20_000_000_000, bytes_accessed=1, transcendentals=0),
        )(sunlit, field, east_courant, north_courant, mixing, *halos, *weights)
        field, edges, weights = outs[0], outs[1:5], outs[5:]
    return field


def solution(mesh):
    placed = (
        P(None, None, "lat", "lon"),
        P(None, "lat", "lon"),
        P(None, "lat", "lon"),
        P(None, "lat", "lon"),
        P("lat", "lon"),
        P(),
        P(),
        P(),
        P(),
        P(),
        P(),
    )
    return jax.shard_map(
        on_device,
        mesh=mesh,
        in_specs=placed,
        out_specs=P(None, None, "lat", "lon"),
        check_vma=False,
    )
```

profile of v0, /device:TPU:0, one launch (start us, length us, event | category | flops | bytes accessed | tf_op | source)
XLA Modules:
  0.0 47.2 jit_solution(11697249461540456388)
XLA Ops:
  0.0 0.0 copy-start.5
  0.0 0.0 copy-start.4
  0.0 0.0 copy-start
  0.0 0.0 copy-start.10
  0.0 0.0 copy-start.6
  0.0 0.0 copy-start.9
  0.0 0.0 copy-start.8
  0.0 0.0 copy-start.3
  0.0 0.0 copy-start.2
  0.1 0.0 copy-start.1
  0.1 0.0 copy-start.7
  0.1 3.1 %first_sends.1 = (f32[32,128]{1,0:T(8,128)}, f32[32,128]{1,0:T(8,128)}, bf16[8,32,128]{2,1,0:T(8,128)(2,1)}, bf16[8,32,128]{2,1,0:T(8,128)(2,1)}) custom-call(f32[32,8,16,128]{3,2,1,0:T(8,128)} %field.1, f32[8,16,128]{2,1,0:T(8,128)} %east_c.5, f32[8,16,128]{2,1,0:T(8,128)} %north_c.5), custom_call_target="tpu_custom_call" | custom-call | flops 4000000000 | bytes 2000000 | tf_op jit(solution)/shard_map/first_sends/pallas_call | solution.py:343
  3.2 0.5 %collective-permute-start.2 = (bf16[8,32,128]{2,1,0:T(8,128)(2,1)}, bf16[8,32,128]{2,1,0:T(8,128)(2,1)S(1)}, u32[]{:S(2)}, u32[]{:S(2)}) collective-permute-start(bf16[8,32,128]{2,1,0:T(8,128)(2,1)} %get-tuple-element.18), channel_id=1, source_target_pairs={{0,8},{8,16},{16,24},{24,0},{1,9},{9,17},{17,25},{25,1},{2,10},{10... | collective-permute-start | bytes 196616 | tf_op jit(solution)/shard_map/ppermute | solution.py:315
  3.7 2.0 %collective-permute-start.3 = (bf16[8,32,128]{2,1,0:T(8,128)(2,1)}, bf16[8,32,128]{2,1,0:T(8,128)(2,1)S(1)}, u32[]{:S(2)}, u32[]{:S(2)}) collective-permute-start(bf16[8,32,128]{2,1,0:T(8,128)(2,1)} %get-tuple-element.19), channel_id=1, source_target_pairs={{8,0},{16,8},{24,16},{0,24},{9,1},{17,9},{25,17},{1,25},{10,2},{18... | collective-permute-start | bytes 196616 | tf_op jit(solution)/shard_map/ppermute | solution.py:316
  5.7 2.3 %collective-permute-start = (f32[32,128]{1,0:T(8,128)}, f32[32,128]{1,0:T(8,128)S(1)}, u32[]{:S(2)}, u32[]{:S(2)}) collective-permute-start(f32[32,128]{1,0:T(8,128)} %get-tuple-element.16), channel_id=1, source_target_pairs={{0,1},{1,2},{2,3},{3,4},{4,5},{5,6},{6,7},{7,0},{8,9},{9,10},{10,1... | collective-permute-start | bytes 49160 | tf_op jit(solution)/shard_map/ppermute | solution.py:317
  7.9 3.0 %collective-permute-start.1 = (f32[32,128]{1,0:T(8,128)}, f32[32,128]{1,0:T(8,128)S(1)}, u32[]{:S(2)}, u32[]{:S(2)}) collective-permute-start(f32[32,128]{1,0:T(8,128)} %get-tuple-element.17), channel_id=1, source_target_pairs={{1,0},{2,1},{3,2},{4,3},{5,4},{6,5},{7,6},{0,7},{9,8},{10,9},{11,1... | collective-permute-start | bytes 49160 | tf_op jit(solution)/shard_map/ppermute | solution.py:318
  11.0 1.9 %collective-permute-done.west_in = f32[32,128]{1,0:T(8,128)S(1)} collective-permute-done((f32[32,128]{1,0:T(8,128)}, f32[32,128]{1,0:T(8,128)S(1)}, u32[]{:S(2)}, u32[]{:S(2)}) %collective-permute-start) | collective-permute-done | bytes 16416 | tf_op jit(solution)/shard_map/ppermute | solution.py:317
  12.9 0.0 collective-permute-done.1.east_in
  12.9 0.0 collective-permute-done.2.south_in
  12.9 0.0 collective-permute-done.3.north_in
  12.9 0.0 copy-done.5
  12.9 0.0 copy-done.4
  12.9 0.0 copy-done
  12.9 0.0 copy-done.10
  13.0 0.0 copy-done.6
  13.0 0.0 copy-done.9
  13.0 0.0 copy-done.8
  13.0 0.0 copy-done.3
  13.0 0.0 copy-done.2
  13.0 0.0 copy-done.1
  13.0 0.0 copy-done.7
  13.0 12.6 %splitting_step.2 = (f32[8,16,32,128]{3,2,1,0:T(8,128)S(1)}, f32[32,128]{1,0:T(8,128)S(1)}, f32[32,128]{1,0:T(8,128)S(1)}, bf16[8,32,128]{2,1,0:T(8,128)(2,1)S(1...) custom-call(s32[1,8]{1,0:T(1,128)S(1)} %copy-done.10, ...), custom_call_target="tpu_custom_call" | custom-call | flops 20000000000 | bytes 1 | tf_op jit(solution)/shard_map/splitting_step/pallas_call | solution.py:377
  25.7 0.1 collective-permute-start.6
  25.7 1.7 %collective-permute-start.7 = (bf16[8,32,128]{2,1,0:T(8,128)(2,1)S(1)}, bf16[8,32,128]{2,1,0:T(8,128)(2,1)S(1)}, u32[]{:S(2)}, u32[]{:S(2)}) collective-permute-start(bf16[8,32,128]{2,1,0:T(8,128)(2,1)S(1)} %get-tuple-element.24), channel_id=1, source_target_pairs={{8,0},{16,8},{24,16},{0,24},{9,1},{17,9},{25,17},{1,25},{10,2},{18... | collective-permute-start | bytes 196616 | tf_op jit(solution)/shard_map/ppermute | solution.py:316
  27.5 1.4 %collective-permute-start.4 = (f32[32,128]{1,0:T(8,128)S(1)}, f32[32,128]{1,0:T(8,128)S(1)}, u32[]{:S(2)}, u32[]{:S(2)}) collective-permute-start(f32[32,128]{1,0:T(8,128)S(1)} %get-tuple-element.21), channel_id=1, source_target_pairs={{0,1},{1,2},{2,3},{3,4},{4,5},{5,6},{6,7},{7,0},{8,9},{9,10},{10,1... | collective-permute-start | bytes 49160 | tf_op jit(solution)/shard_map/ppermute | solution.py:317
  28.9 3.3 %collective-permute-start.5 = (f32[32,128]{1,0:T(8,128)S(1)}, f32[32,128]{1,0:T(8,128)S(1)}, u32[]{:S(2)}, u32[]{:S(2)}) collective-permute-start(f32[32,128]{1,0:T(8,128)S(1)} %get-tuple-element.22), channel_id=1, source_target_pairs={{1,0},{2,1},{3,2},{4,3},{5,4},{6,5},{7,6},{0,7},{9,8},{10,9},{11,1... | collective-permute-start | bytes 49160 | tf_op jit(solution)/shard_map/ppermute | solution.py:318
  32.2 1.7 %collective-permute-done.4.west_in = f32[32,128]{1,0:T(8,128)S(1)} collective-permute-done((f32[32,128]{1,0:T(8,128)S(1)}, f32[32,128]{1,0:T(8,128)S(1)}, u32[]{:S(2)}, u32[]{:S(2)}) %collective-permute-start.4) | collective-permute-done | bytes 16416 | tf_op jit(solution)/shard_map/ppermute | solution.py:317
  33.9 0.0 collective-permute-done.5.east_in
  33.9 0.0 collective-permute-done.6.south_in
  33.9 0.0 collective-permute-done.7.north_in
  33.9 13.3 %splitting_step.3 = f32[32,8,16,128]{3,2,1,0:T(8,128)} custom-call(s32[1,8]{1,0:T(1,128)S(1)} %copy-done.10, f32[8,16,32,128]{3,2,1,0:T(8,128)S(1)} %get-tuple-element.20.field, f32[8,16,128]{2,1,0:T(8,128)S(1)} %copy-done.4, f32[8,16,128]{2,1,0:T(8,128)S(1)} %copy-done.5, f32[7,16,128]{2,1,0:T(8,128)S(1)} %copy-done.6, ...), custom_call_target="tpu_custom_call" | custom-call | flops 20000000000 | bytes 1 | tf_op jit(solution)/shard_map/splitting_step/pallas_call | solution.py:377
Async XLA Ops:
  0.0 12.9 %copy-start.5 = (f32[8,16,128]{2,1,0:T(8,128)S(1)}, f32[8,16,128]{2,1,0:T(8,128)}, u32[]{:S(2)}) copy-start(f32[8,16,128]{2,1,0:T(8,128)} %north_c.5) | copy-start | bytes 196612
  0.0 12.9 %copy-start.4 = (f32[8,16,128]{2,1,0:T(8,128)S(1)}, f32[8,16,128]{2,1,0:T(8,128)}, u32[]{:S(2)}) copy-start(f32[8,16,128]{2,1,0:T(8,128)} %east_c.5) | copy-start | bytes 196612
  0.0 12.9 %copy-start = (f32[32,8,16,128]{3,2,1,0:T(8,128)S(1)}, f32[32,8,16,128]{3,2,1,0:T(8,128)}, u32[]{:S(2)}) copy-start(f32[32,8,16,128]{3,2,1,0:T(8,128)} %field.1) | copy-start | bytes 6291460
  0.0 12.9 %copy-start.10 = (s32[1,8]{1,0:T(1,128)S(1)}, s32[1,8]{1,0:T(1,128)}, u32[]{:S(2)}) copy-start(s32[1,8]{1,0:T(1,128)} %sun.3) | copy-start | bytes 100
  0.0 12.9 %copy-start.6 = (f32[7,16,128]{2,1,0:T(8,128)S(1)}, f32[7,16,128]{2,1,0:T(8,128)}, u32[]{:S(2)}) copy-start(f32[7,16,128]{2,1,0:T(8,128)} %mixing.3) | copy-start | bytes 172036
  0.0 13.0 %copy-start.9 = (f32[256]{0:T(256)S(1)}, f32[256]{0:T(256)}, u32[]{:S(2)}) copy-start(f32[256]{0:T(256)} %param.21) | copy-start | bytes 3076
  0.0 13.0 %copy-start.8 = (bf16[32,224]{1,0:T(8,128)(2,1)S(1)}, bf16[32,224]{1,0:T(8,128)(2,1)}, u32[]{:S(2)}) copy-start(bf16[32,224]{1,0:T(8,128)(2,1)} %refs_4_.1) | copy-start | bytes 43012
  0.0 13.0 %copy-start.3 = (bf16[224,256]{1,0:T(8,128)(2,1)S(1)}, bf16[224,256]{1,0:T(8,128)(2,1)}, u32[]{:S(2)}) copy-start(bf16[224,256]{1,0:T(8,128)(2,1)} %refs_3_.1) | copy-start | bytes 344068
  0.0 13.0 %copy-start.2 = (bf16[256,224]{0,1:T(8,128)(2,1)S(1)}, bf16[256,224]{0,1:T(8,128)(2,1)}, u32[]{:S(2)}) copy-start(bf16[256,224]{0,1:T(8,128)(2,1)} %param.18) | copy-start | bytes 344068
  0.1 13.0 %copy-start.1 = (bf16[256,224]{0,1:T(8,128)(2,1)S(1)}, bf16[256,224]{0,1:T(8,128)(2,1)}, u32[]{:S(2)}) copy-start(bf16[256,224]{0,1:T(8,128)(2,1)} %param.17) | copy-start | bytes 344068
  0.1 13.0 %copy-start.7 = (bf16[224,32]{0,1:T(8,128)(2,1)S(1)}, bf16[224,32]{0,1:T(8,128)(2,1)}, u32[]{:S(2)}) copy-start(bf16[224,32]{0,1:T(8,128)(2,1)} %param.16) | copy-start | bytes 43012
  3.2 9.8 %collective-permute-start.2 = (bf16[8,32,128]{2,1,0:T(8,128)(2,1)}, bf16[8,32,128]{2,1,0:T(8,128)(2,1)S(1)}, u32[]{:S(2)}, u32[]{:S(2)}) collective-permute-start(bf16[8,32,128]{2,1,0:T(8,128)(2,1)} %get-tuple-element.18), channel_id=1, source_target_pairs={{0,8},{8,16},{16,24},{24,0},{1,9},{9,17},{17,25},{25,1},{2,10},{10... | collective-permute-start | bytes 196616 | tf_op jit(solution)/shard_map/ppermute | solution.py:315
  3.7 9.2 %collective-permute-start.3 = (bf16[8,32,128]{2,1,0:T(8,128)(2,1)}, bf16[8,32,128]{2,1,0:T(8,128)(2,1)S(1)}, u32[]{:S(2)}, u32[]{:S(2)}) collective-permute-start(bf16[8,32,128]{2,1,0:T(8,128)(2,1)} %get-tuple-element.19), channel_id=1, source_target_pairs={{8,0},{16,8},{24,16},{0,24},{9,1},{17,9},{25,17},{1,25},{10,2},{18... | collective-permute-start | bytes 196616 | tf_op jit(solution)/shard_map/ppermute | solution.py:316
  5.7 7.2 %collective-permute-start = (f32[32,128]{1,0:T(8,128)}, f32[32,128]{1,0:T(8,128)S(1)}, u32[]{:S(2)}, u32[]{:S(2)}) collective-permute-start(f32[32,128]{1,0:T(8,128)} %get-tuple-element.16), channel_id=1, source_target_pairs={{0,1},{1,2},{2,3},{3,4},{4,5},{5,6},{6,7},{7,0},{8,9},{9,10},{10,1... | collective-permute-start | bytes 49160 | tf_op jit(solution)/shard_map/ppermute | solution.py:317
  7.9 5.0 %collective-permute-start.1 = (f32[32,128]{1,0:T(8,128)}, f32[32,128]{1,0:T(8,128)S(1)}, u32[]{:S(2)}, u32[]{:S(2)}) collective-permute-start(f32[32,128]{1,0:T(8,128)} %get-tuple-element.17), channel_id=1, source_target_pairs={{1,0},{2,1},{3,2},{4,3},{5,4},{6,5},{7,6},{0,7},{9,8},{10,9},{11,1... | collective-permute-start | bytes 49160 | tf_op jit(solution)/shard_map/ppermute | solution.py:318
  25.7 8.2 %collective-permute-start.6 = (bf16[8,32,128]{2,1,0:T(8,128)(2,1)S(1)}, bf16[8,32,128]{2,1,0:T(8,128)(2,1)S(1)}, u32[]{:S(2)}, u32[]{:S(2)}) collective-permute-start(bf16[8,32,128]{2,1,0:T(8,128)(2,1)S(1)} %get-tuple-element.23), channel_id=1, source_target_pairs={{0,8},{8,16},{16,24},{24,0},{1,9},{9,17},{17,25},{25,1},{2,10},{10... | collective-permute-start | bytes 196616 | tf_op jit(solution)/shard_map/ppermute | solution.py:315
  25.7 8.2 %collective-permute-start.7 = (bf16[8,32,128]{2,1,0:T(8,128)(2,1)S(1)}, bf16[8,32,128]{2,1,0:T(8,128)(2,1)S(1)}, u32[]{:S(2)}, u32[]{:S(2)}) collective-permute-start(bf16[8,32,128]{2,1,0:T(8,128)(2,1)S(1)} %get-tuple-element.24), channel_id=1, source_target_pairs={{8,0},{16,8},{24,16},{0,24},{9,1},{17,9},{25,17},{1,25},{10,2},{18... | collective-permute-start | bytes 196616 | tf_op jit(solution)/shard_map/ppermute | solution.py:316
  27.5 6.4 %collective-permute-start.4 = (f32[32,128]{1,0:T(8,128)S(1)}, f32[32,128]{1,0:T(8,128)S(1)}, u32[]{:S(2)}, u32[]{:S(2)}) collective-permute-start(f32[32,128]{1,0:T(8,128)S(1)} %get-tuple-element.21), channel_id=1, source_target_pairs={{0,1},{1,2},{2,3},{3,4},{4,5},{5,6},{6,7},{7,0},{8,9},{9,10},{10,1... | collective-permute-start | bytes 49160 | tf_op jit(solution)/shard_map/ppermute | solution.py:317
  28.9 5.0 %collective-permute-start.5 = (f32[32,128]{1,0:T(8,128)S(1)}, f32[32,128]{1,0:T(8,128)S(1)}, u32[]{:S(2)}, u32[]{:S(2)}) collective-permute-start(f32[32,128]{1,0:T(8,128)S(1)} %get-tuple-element.22), channel_id=1, source_target_pairs={{1,0},{2,1},{3,2},{4,3},{5,4},{6,5},{7,6},{0,7},{9,8},{10,9},{11,1... | collective-permute-start | bytes 49160 | tf_op jit(solution)/shard_map/ppermute | solution.py:318
where the time goes:
time: 47.3 us; the launch traced here: 47.2 us
  Pallas kernels  29 us (61%)
  starting transfers between devices  14.3 us (30%)
  waiting for transfers between devices  3.65 us (8%)
    pallas_call x2, Pallas kernels, on_device(): pl.pallas_call(functools.partial(step_kernel, n_levels, n_rows, first, la...  25.9 us
    ppermute x2, starting transfers between devices, exchanged(): from_east = lax.ppermute(west, 'lon', down)  6.37 us
    ppermute x2, starting transfers between devices, exchanged(): from_north = lax.ppermute(south, 'lat', descend)  3.72 us
    ppermute x2, starting transfers between devices, exchanged(): from_west = lax.ppermute(east, 'lon', up)  3.66 us
    ppermute x2, waiting for transfers between devices, exchanged(): from_west = lax.ppermute(east, 'lon', up)  3.63 us
    pallas_call x1, Pallas kernels, on_device(): pl.pallas_call(first_kernel, out_shape=(side, side, edge, edge), in_specs...  3.07 us
  transfers between devices with their start and end apart: 8, of which 2 were waited for; matrix products, arithmetic and copies ran while one was open for 0% of the time, Pallas kernels for 0%

commit v1 on v0

--- a/solution.py
+++ b/solution.py
@@ -47,6 +47,16 @@
     return index == 0, index == lax.axis_size("lat") - 1
 
 
+def is_even(axis):
+    return lax.axis_index(axis) % 2 == 0
+
+
+def by_parity(axis, up, down, into_first, into_second):
+    even = is_even(axis)
+    into_first[...] = jnp.where(even, up, down)
+    into_second[...] = jnp.where(even, down, up)
+
+
 def pack_sides(value, coef, at, west, east):
     lanes = lane_ids(value.shape)
     size = value.shape[-1]
@@ -56,7 +66,7 @@
     return west, east
 
 
-def first_kernel(latent, east_c, north_c, west, east, south, north, *scratch):
+def first_kernel(latent, east_c, north_c, lon_a, lon_b, lat_a, lat_b, *scratch):
     tiles, east_v, north_v, sems = scratch
     n_levels, n_species, n_rows, n_cols = tiles.shape
     lanes = lane_ids((1, n_cols))
@@ -83,11 +93,12 @@
             speed = east_v[level, r : r + 1, :]
             coef = jnp.where(lanes == 0, jnp.minimum(speed, 0.0), jnp.maximum(speed, 0.0))
             sides = pack_sides(value, coef, at, *sides)
-        for r, out, clip in ((0, south, jnp.minimum), (n_rows - 1, north, jnp.maximum)):
+        ends = []
+        for r, closed, clip in ((0, is_first, jnp.minimum), (n_rows - 1, is_last, jnp.maximum)):
             speed = clip(north_v[level, r : r + 1, :], 0.0)
-            speed = jnp.where(is_first if r == 0 else is_last, 0.0, speed)
-            out[level] = (tile[r] * speed).astype(BF16)
-    west[...], east[...] = sides
+            ends.append((tile[r] * jnp.where(closed, 0.0, speed)).astype(BF16))
+        by_parity("lat", ends[1], ends[0], lat_a.at[level], lat_b.at[level])
+    by_parity("lon", sides[1], sides[0], lon_a, lon_b)
 
 
 def step_kernel(
@@ -100,10 +111,10 @@
     east_c,
     north_c,
     mixing,
-    west_in,
-    east_in,
-    south_in,
-    north_in,
+    lon_a_in,
+    lon_b_in,
+    lat_a_in,
+    lat_b_in,
     *refs,
 ):
     if first:
@@ -112,10 +123,11 @@
     else:
         (linear, encode), refs = refs[:2], refs[2:]
     half_rows = n_rows // 2
+    south_in, north_in, west_in, east_in, coefs, diffused = refs[-6:]
     if last:
-        coefs, diffused, staged, sems = refs[-4:]
-    else:
-        coefs, diffused = refs[-2:]
+        staged, sems = refs[-8:-6]
+    by_parity("lon", lon_a_in[...], lon_b_in[...], east_in, west_in)
+    by_parity("lat", lat_a_in[...], lat_b_in[...], north_in, south_in)
     n_species, n_cols = west_in.shape
     n_reactions = encode.shape[1]
     cells = n_levels * n_rows
@@ -123,7 +135,7 @@
     row_ids = lax.broadcasted_iota(jnp.int32, (n_rows, n_cols), 0)
     is_first, is_last = at_ends()
     if first:
-        latent, field = field, refs[-3]
+        latent, field = field, refs[-7]
         fold_weights(*weights, linear, encode)
         for level in range(n_levels):
             field[level] = jnp.transpose(latent[:, level], (1, 0, 2))
@@ -294,29 +306,28 @@
         for copy in copies:
             copy.wait()
         return
-    out, west, east, south, north = refs[:5]
+    out, lon_a, lon_b, lat_a, lat_b = refs[:5]
     zeros = jnp.zeros((n_species, n_cols), F32)
-    west[...], east[...] = lax.fori_loop(0, n_groups, rows, (zeros, zeros))
+    west, east = lax.fori_loop(0, n_groups, rows, (zeros, zeros))
+    by_parity("lon", east, west, lon_a, lon_b)
     for level in range(n_levels):
-        for edge, send, kind in ((0, south, SOUTH), (n_rows - 1, north, NORTH)):
-            send[level] = (out[level, edge] * coefs[kind, level, edge : edge + 1]).astype(BF16)
+        south = (out[level, 0] * coefs[SOUTH, level, :1]).astype(BF16)
+        north = (out[level, n_rows - 1] * coefs[NORTH, level, n_rows - 1 :]).astype(BF16)
+        by_parity("lat", north, south, lat_a.at[level], lat_b.at[level])
 
 
 def vmem(count):
     return [pl.BlockSpec(memory_space=pltpu.VMEM)] * count
 
 
-def exchanged(west, east, south, north):
-    lon, lat = lax.axis_size("lon"), lax.axis_size("lat")
-    up = [(i, (i + 1) % lon) for i in range(lon)]
-    down = [(j, i) for i, j in up]
-    climb = [(i, (i + 1) % lat) for i in range(lat)]
-    descend = [(j, i) for i, j in climb]
-    from_south = lax.ppermute(north, "lat", climb)
-    from_north = lax.ppermute(south, "lat", descend)
-    from_west = lax.ppermute(east, "lon", up)
-    from_east = lax.ppermute(west, "lon", down)
-    return from_west, from_east, from_south, from_north
+def exchanged(lon_a, lon_b, lat_a, lat_b):
+    def swapped(array, axis, first):
+        size = lax.axis_size(axis)
+        pairs = [(i % size, (i + 1) % size) for i in range(first, size + first, 2)]
+        return lax.ppermute(array, axis, pairs + [(j, i) for i, j in pairs])
+
+    lat_a, lat_b = swapped(lat_a, "lat", 0), swapped(lat_b, "lat", 1)
+    return swapped(lon_a, "lon", 0), swapped(lon_b, "lon", 1), lat_a, lat_b
 
 
 def on_device(
@@ -365,15 +376,16 @@
         first, last = step == 0, step == STEPS - 1
         halos = exchanged(*edges)
         scratch = [pltpu.VMEM(layered.shape, F32)] if first else []
-        scratch += [
-            pltpu.VMEM((8, n_levels, n_rows, n_cols), F32),
-            pltpu.VMEM((n_levels, n_rows + ROWS_AT_ONCE, n_species, n_cols), F32),
-        ]
         if last:
             scratch += [
                 pltpu.VMEM((2, n_levels, n_species, n_rows // 2, n_cols), F32),
                 pltpu.SemaphoreType.DMA((2, n_levels)),
             ]
+        scratch += [pltpu.VMEM(array.shape, array.dtype) for array in (edge, edge, side, side)]
+        scratch += [
+            pltpu.VMEM((8, n_levels, n_rows, n_cols), F32),
+            pltpu.VMEM((n_levels, n_rows + ROWS_AT_ONCE, n_species, n_cols), F32),
+        ]
         outs = pl.pallas_call(
             functools.partial(step_kernel, n_levels, n_rows, first, last),
             out_shape=(jax.ShapeDtypeStruct(latent_field.shape, F32),)

time: 47.3 us -> 47.7 us (level)
  waiting for transfers between devices: 3.65 us -> 6 us
  starting transfers between devices: 14.3 us -> 12.5 us
    ppermute x8, waiting for transfers between devices: 3.65 us -> 6 us  [swapped(): return lax.ppermute(array, axis, pairs + [(j, i) for i, j in pairs])]
    ppermute x8, starting transfers between devices: 14.3 us -> 12.5 us  [swapped(): return lax.ppermute(array, axis, pairs + [(j, i) for i, j in pairs])]
  transfers between devices with their start and end apart: 8 -> 8, of which waited for: 2 -> 3; matrix products, arithmetic and copies ran while one was open for 0% -> 0% of each run, Pallas kernels for 0% -> 0%
where the time goes in v1:
time: 47.7 us; the launch traced here: 47.6 us
  Pallas kernels  28.9 us (61%)
  starting transfers between devices  12.5 us (26%)
  waiting for transfers between devices  6 us (13%)
    pallas_call x2, Pallas kernels, on_device(): pl.pallas_call(functools.partial(step_kernel, n_levels, n_rows, first, la...  25.8 us
    ppermute x8, starting transfers between devices, swapped(): return lax.ppermute(array, axis, pairs + [(j, i) for i, j in pairs])  12.5 us
    ppermute x8, waiting for transfers between devices, swapped(): return lax.ppermute(array, axis, pairs + [(j, i) for i, j in pairs])  6 us
    pallas_call x1, Pallas kernels, on_device(): pl.pallas_call(first_kernel, out_shape=(side, side, edge, edge), in_specs...  3.07 us
  transfers between devices with their start and end apart: 8, of which 3 were waited for; matrix products, arithmetic and copies ran while one was open for 0% of the time, Pallas kernels for 0%

profile of v1, /device:TPU:0, one launch (start us, length us, event | category | flops | bytes accessed | tf_op | source)
XLA Modules:
  0.0 47.6 jit_solution(252165525315669377)
XLA Ops:
  0.0 0.0 copy-start.5
  0.0 0.0 copy-start.4
  0.0 0.0 copy-start
  0.0 0.0 copy-start.10
  0.0 0.0 copy-start.6
  0.0 0.0 copy-start.9
  0.0 0.0 copy-start.8
  0.0 0.0 copy-start.3
  0.0 0.0 copy-start.2
  0.1 0.0 copy-start.1
  0.1 0.0 copy-start.7
  0.1 3.1 %first_sends.1 = (f32[32,128]{1,0:T(8,128)}, f32[32,128]{1,0:T(8,128)}, bf16[8,32,128]{2,1,0:T(8,128)(2,1)}, bf16[8,32,128]{2,1,0:T(8,128)(2,1)}) custom-call(f32[32,8,16,128]{3,2,1,0:T(8,128)} %field.1, f32[8,16,128]{2,1,0:T(8,128)} %east_c.5, f32[8,16,128]{2,1,0:T(8,128)} %north_c.5), custom_call_target="tpu_custom_call" | custom-call | flops 4000000000 | bytes 2000000 | tf_op jit(solution)/shard_map/first_sends/pallas_call | solution.py:354
  3.2 0.5 %collective-permute-start.2 = (bf16[8,32,128]{2,1,0:T(8,128)(2,1)}, bf16[8,32,128]{2,1,0:T(8,128)(2,1)S(1)}, u32[]{:S(2)}, u32[]{:S(2)}) collective-permute-start(bf16[8,32,128]{2,1,0:T(8,128)(2,1)} %get-tuple-element.18), channel_id=1, source_target_pairs={{0,8},{16,24},{8,0},{24,16},{1,9},{17,25},{9,1},{25,17},{2,10},{18... | collective-permute-start | bytes 196616 | tf_op jit(solution)/shard_map/ppermute | solution.py:327
  3.7 2.6 %collective-permute-start.3 = (bf16[8,32,128]{2,1,0:T(8,128)(2,1)}, bf16[8,32,128]{2,1,0:T(8,128)(2,1)S(1)}, u32[]{:S(2)}, u32[]{:S(2)}) collective-permute-start(bf16[8,32,128]{2,1,0:T(8,128)(2,1)} %get-tuple-element.19), channel_id=1, source_target_pairs={{8,16},{24,0},{16,8},{0,24},{9,17},{25,1},{17,9},{1,25},{10,18},{2... | collective-permute-start | bytes 196616 | tf_op jit(solution)/shard_map/ppermute | solution.py:327
  6.3 1.5 %collective-permute-start = (f32[32,128]{1,0:T(8,128)}, f32[32,128]{1,0:T(8,128)S(1)}, u32[]{:S(2)}, u32[]{:S(2)}) collective-permute-start(f32[32,128]{1,0:T(8,128)} %get-tuple-element.16), channel_id=1, source_target_pairs={{0,1},{2,3},{4,5},{6,7},{1,0},{3,2},{5,4},{7,6},{8,9},{10,11},{12,... | collective-permute-start | bytes 49160 | tf_op jit(solution)/shard_map/ppermute | solution.py:327
  7.8 3.5 %collective-permute-start.1 = (f32[32,128]{1,0:T(8,128)}, f32[32,128]{1,0:T(8,128)S(1)}, u32[]{:S(2)}, u32[]{:S(2)}) collective-permute-start(f32[32,128]{1,0:T(8,128)} %get-tuple-element.17), channel_id=1, source_target_pairs={{1,2},{3,4},{5,6},{7,0},{2,1},{4,3},{6,5},{0,7},{9,10},{11,12},{13... | collective-permute-start | bytes 49160 | tf_op jit(solution)/shard_map/ppermute | solution.py:327
  11.4 0.0 collective-permute-done.lon_a_in
  11.4 3.1 %collective-permute-done.1.lon_b_in = f32[32,128]{1,0:T(8,128)S(1)} collective-permute-done((f32[32,128]{1,0:T(8,128)}, f32[32,128]{1,0:T(8,128)S(1)}, u32[]{:S(2)}, u32[]{:S(2)}) %collective-permute-start.1) | collective-permute-done | bytes 16416 | tf_op jit(solution)/shard_map/ppermute | solution.py:327
  14.5 0.0 collective-permute-done.2.lat_a_in
  14.5 0.0 collective-permute-done.3.lat_b_in
  14.5 0.0 copy-done.5
  14.5 0.0 copy-done.4
  14.5 0.0 copy-done
  14.5 0.0 copy-done.10
  14.5 0.0 copy-done.6
  14.5 0.0 copy-done.9
  14.5 0.0 copy-done.8
  14.5 0.0 copy-done.3
  14.6 0.0 copy-done.2
  14.6 0.0 copy-done.1
  14.6 0.0 copy-done.7
  14.6 12.5 %splitting_step.2 = (f32[8,16,32,128]{3,2,1,0:T(8,128)S(1)}, f32[32,128]{1,0:T(8,128)S(1)}, f32[32,128]{1,0:T(8,128)S(1)}, bf16[8,32,128]{2,1,0:T(8,128)(2,1)S(1...) custom-call(s32[1,8]{1,0:T(1,128)S(1)} %copy-done.10, ...), custom_call_target="tpu_custom_call" | custom-call | flops 20000000000 | bytes 1 | tf_op jit(solution)/shard_map/splitting_step/pallas_call | solution.py:389
  27.1 0.1 collective-permute-start.6
  27.2 0.6 %collective-permute-start.7 = (bf16[8,32,128]{2,1,0:T(8,128)(2,1)S(1)}, bf16[8,32,128]{2,1,0:T(8,128)(2,1)S(1)}, u32[]{:S(2)}, u32[]{:S(2)}) collective-permute-start(bf16[8,32,128]{2,1,0:T(8,128)(2,1)S(1)} %get-tuple-element.24), channel_id=1, source_target_pairs={{8,16},{24,0},{16,8},{0,24},{9,17},{25,1},{17,9},{1,25},{10,18},{2... | collective-permute-start | bytes 196616 | tf_op jit(solution)/shard_map/ppermute | solution.py:327
  27.8 0.0 collective-permute-start.4
  27.8 3.5 %collective-permute-start.5 = (f32[32,128]{1,0:T(8,128)S(1)}, f32[32,128]{1,0:T(8,128)S(1)}, u32[]{:S(2)}, u32[]{:S(2)}) collective-permute-start(f32[32,128]{1,0:T(8,128)S(1)} %get-tuple-element.22), channel_id=1, source_target_pairs={{1,2},{3,4},{5,6},{7,0},{2,1},{4,3},{6,5},{0,7},{9,10},{11,12},{13... | collective-permute-start | bytes 49160 | tf_op jit(solution)/shard_map/ppermute | solution.py:327
  31.4 0.2 collective-permute-done.4.lon_a_in
  31.6 2.7 %collective-permute-done.5.lon_b_in = f32[32,128]{1,0:T(8,128)S(1)} collective-permute-done((f32[32,128]{1,0:T(8,128)S(1)}, f32[32,128]{1,0:T(8,128)S(1)}, u32[]{:S(2)}, u32[]{:S(2)}) %collective-permute-start.5) | collective-permute-done | bytes 16416 | tf_op jit(solution)/shard_map/ppermute | solution.py:327
  34.3 0.0 collective-permute-done.6.lat_a_in
  34.3 0.0 collective-permute-done.7.lat_b_in
  34.3 13.3 %splitting_step.3 = f32[32,8,16,128]{3,2,1,0:T(8,128)} custom-call(s32[1,8]{1,0:T(1,128)S(1)} %copy-done.10, f32[8,16,32,128]{3,2,1,0:T(8,128)S(1)} %get-tuple-element.20.field, f32[8,16,128]{2,1,0:T(8,128)S(1)} %copy-done.4, f32[8,16,128]{2,1,0:T(8,128)S(1)} %copy-done.5, f32[7,16,128]{2,1,0:T(8,128)S(1)} %copy-done.6, ...), custom_call_target="tpu_custom_call" | custom-call | flops 20000000000 | bytes 1 | tf_op jit(solution)/shard_map/splitting_step/pallas_call | solution.py:389
Async XLA Ops:
  0.0 14.5 %copy-start.5 = (f32[8,16,128]{2,1,0:T(8,128)S(1)}, f32[8,16,128]{2,1,0:T(8,128)}, u32[]{:S(2)}) copy-start(f32[8,16,128]{2,1,0:T(8,128)} %north_c.5) | copy-start | bytes 196612
  0.0 14.5 %copy-start.4 = (f32[8,16,128]{2,1,0:T(8,128)S(1)}, f32[8,16,128]{2,1,0:T(8,128)}, u32[]{:S(2)}) copy-start(f32[8,16,128]{2,1,0:T(8,128)} %east_c.5) | copy-start | bytes 196612
  0.0 14.5 %copy-start = (f32[32,8,16,128]{3,2,1,0:T(8,128)S(1)}, f32[32,8,16,128]{3,2,1,0:T(8,128)}, u32[]{:S(2)}) copy-start(f32[32,8,16,128]{3,2,1,0:T(8,128)} %field.1) | copy-start | bytes 6291460
  0.0 14.5 %copy-start.10 = (s32[1,8]{1,0:T(1,128)S(1)}, s32[1,8]{1,0:T(1,128)}, u32[]{:S(2)}) copy-start(s32[1,8]{1,0:T(1,128)} %sun.3) | copy-start | bytes 100
  0.0 14.5 %copy-start.6 = (f32[7,16,128]{2,1,0:T(8,128)S(1)}, f32[7,16,128]{2,1,0:T(8,128)}, u32[]{:S(2)}) copy-start(f32[7,16,128]{2,1,0:T(8,128)} %mixing.3) | copy-start | bytes 172036
  0.0 14.5 %copy-start.9 = (f32[256]{0:T(256)S(1)}, f32[256]{0:T(256)}, u32[]{:S(2)}) copy-start(f32[256]{0:T(256)} %param.21) | copy-start | bytes 3076
  0.0 14.5 %copy-start.8 = (bf16[32,224]{1,0:T(8,128)(2,1)S(1)}, bf16[32,224]{1,0:T(8,128)(2,1)}, u32[]{:S(2)}) copy-start(bf16[32,224]{1,0:T(8,128)(2,1)} %refs_4_.1) | copy-start | bytes 43012
  0.0 14.5 %copy-start.3 = (bf16[224,256]{1,0:T(8,128)(2,1)S(1)}, bf16[224,256]{1,0:T(8,128)(2,1)}, u32[]{:S(2)}) copy-start(bf16[224,256]{1,0:T(8,128)(2,1)} %refs_3_.1) | copy-start | bytes 344068
  0.0 14.5 %copy-start.2 = (bf16[256,224]{0,1:T(8,128)(2,1)S(1)}, bf16[256,224]{0,1:T(8,128)(2,1)}, u32[]{:S(2)}) copy-start(bf16[256,224]{0,1:T(8,128)(2,1)} %param.18) | copy-start | bytes 344068
  0.1 14.5 %copy-start.1 = (bf16[256,224]{0,1:T(8,128)(2,1)S(1)}, bf16[256,224]{0,1:T(8,128)(2,1)}, u32[]{:S(2)}) copy-start(bf16[256,224]{0,1:T(8,128)(2,1)} %param.17) | copy-start | bytes 344068
  0.1 14.5 %copy-start.7 = (bf16[224,32]{0,1:T(8,128)(2,1)S(1)}, bf16[224,32]{0,1:T(8,128)(2,1)}, u32[]{:S(2)}) copy-start(bf16[224,32]{0,1:T(8,128)(2,1)} %param.16) | copy-start | bytes 43012
  3.2 11.3 %collective-permute-start.2 = (bf16[8,32,128]{2,1,0:T(8,128)(2,1)}, bf16[8,32,128]{2,1,0:T(8,128)(2,1)S(1)}, u32[]{:S(2)}, u32[]{:S(2)}) collective-permute-start(bf16[8,32,128]{2,1,0:T(8,128)(2,1)} %get-tuple-element.18), channel_id=1, source_target_pairs={{0,8},{16,24},{8,0},{24,16},{1,9},{17,25},{9,1},{25,17},{2,10},{18... | collective-permute-start | bytes 196616 | tf_op jit(solution)/shard_map/ppermute | solution.py:327
  3.7 10.8 %collective-permute-start.3 = (bf16[8,32,128]{2,1,0:T(8,128)(2,1)}, bf16[8,32,128]{2,1,0:T(8,128)(2,1)S(1)}, u32[]{:S(2)}, u32[]{:S(2)}) collective-permute-start(bf16[8,32,128]{2,1,0:T(8,128)(2,1)} %get-tuple-element.19), channel_id=1, source_target_pairs={{8,16},{24,0},{16,8},{0,24},{9,17},{25,1},{17,9},{1,25},{10,18},{2... | collective-permute-start | bytes 196616 | tf_op jit(solution)/shard_map/ppermute | solution.py:327
  6.3 5.1 %collective-permute-start = (f32[32,128]{1,0:T(8,128)}, f32[32,128]{1,0:T(8,128)S(1)}, u32[]{:S(2)}, u32[]{:S(2)}) collective-permute-start(f32[32,128]{1,0:T(8,128)} %get-tuple-element.16), channel_id=1, source_target_pairs={{0,1},{2,3},{4,5},{6,7},{1,0},{3,2},{5,4},{7,6},{8,9},{10,11},{12,... | collective-permute-start | bytes 49160 | tf_op jit(solution)/shard_map/ppermute | solution.py:327
  7.8 6.6 %collective-permute-start.1 = (f32[32,128]{1,0:T(8,128)}, f32[32,128]{1,0:T(8,128)S(1)}, u32[]{:S(2)}, u32[]{:S(2)}) collective-permute-start(f32[32,128]{1,0:T(8,128)} %get-tuple-element.17), channel_id=1, source_target_pairs={{1,2},{3,4},{5,6},{7,0},{2,1},{4,3},{6,5},{0,7},{9,10},{11,12},{13... | collective-permute-start | bytes 49160 | tf_op jit(solution)/shard_map/ppermute | solution.py:327
  27.1 7.2 %collective-permute-start.6 = (bf16[8,32,128]{2,1,0:T(8,128)(2,1)S(1)}, bf16[8,32,128]{2,1,0:T(8,128)(2,1)S(1)}, u32[]{:S(2)}, u32[]{:S(2)}) collective-permute-start(bf16[8,32,128]{2,1,0:T(8,128)(2,1)S(1)} %get-tuple-element.23), channel_id=1, source_target_pairs={{0,8},{16,24},{8,0},{24,16},{1,9},{17,25},{9,1},{25,17},{2,10},{18... | collective-permute-start | bytes 196616 | tf_op jit(solution)/shard_map/ppermute | solution.py:327
  27.2 7.1 %collective-permute-start.7 = (bf16[8,32,128]{2,1,0:T(8,128)(2,1)S(1)}, bf16[8,32,128]{2,1,0:T(8,128)(2,1)S(1)}, u32[]{:S(2)}, u32[]{:S(2)}) collective-permute-start(bf16[8,32,128]{2,1,0:T(8,128)(2,1)S(1)} %get-tuple-element.24), channel_id=1, source_target_pairs={{8,16},{24,0},{16,8},{0,24},{9,17},{25,1},{17,9},{1,25},{10,18},{2... | collective-permute-start | bytes 196616 | tf_op jit(solution)/shard_map/ppermute | solution.py:327
  27.8 3.7 %collective-permute-start.4 = (f32[32,128]{1,0:T(8,128)S(1)}, f32[32,128]{1,0:T(8,128)S(1)}, u32[]{:S(2)}, u32[]{:S(2)}) collective-permute-start(f32[32,128]{1,0:T(8,128)S(1)} %get-tuple-element.21), channel_id=1, source_target_pairs={{0,1},{2,3},{4,5},{6,7},{1,0},{3,2},{5,4},{7,6},{8,9},{10,11},{12,... | collective-permute-start | bytes 49160 | tf_op jit(solution)/shard_map/ppermute | solution.py:327
  27.8 6.4 %collective-permute-start.5 = (f32[32,128]{1,0:T(8,128)S(1)}, f32[32,128]{1,0:T(8,128)S(1)}, u32[]{:S(2)}, u32[]{:S(2)}) collective-permute-start(f32[32,128]{1,0:T(8,128)S(1)} %get-tuple-element.22), channel_id=1, source_target_pairs={{1,2},{3,4},{5,6},{7,0},{2,1},{4,3},{6,5},{0,7},{9,10},{11,12},{13... | collective-permute-start | bytes 49160 | tf_op jit(solution)/shard_map/ppermute | solution.py:327
